TPU v7x, 32 devices: a whole 2x2x4 slice. The times are simulated.
32 devices in a mesh: row: 8 (over z, y), col: 4 (over x, core).
Axes of the slice: x: 2, y: 2, z: 4, core: 2. Of those that a mesh axis runs over, the one named last changes fastest.
Arguments:
- queries: bfloat16 [4096, 1792], P(('row', 'col')), may hold values from -120 to 120, as said below
- keys_values: bfloat16 [4096, 512], P(('row', 'col')), may hold values from -5.5 to 5.5
- segment_ids: int32 [4096], P(('row', 'col')), may hold values from 0 to 7, never falling along the last dimension, each value on 1 to 3072 neighbouring positions
Outputs:
- context: bfloat16 [4096, 1792], P(('row', 'col'))
Inputs may be any that keep to these rules, and one draw needn't show every extreme that they name: `queries`: some query rows may be large multiples of a visible key, so scores reach about 270.
All inputs are finite; a program needn't handle non-finite values.
Results may differ from a plain program's by a relative error of at most 0.017.
Values may be sent and summed in bfloat16 or wider, within the bound.
A program may use at most 128 MiB of HBM per device.

v0:
```python
import functools
import math

import jax
import jax.numpy as jnp
from jax import lax
from jax.experimental import pallas as pl
from jax.experimental.pallas import tpu as pltpu
from jax.sharding import PartitionSpec as P

HD = 128
KVH = 2
BIG = 2.0**100
MESH = pl.DeviceIdType.MESH


def kernel(Z, Y, X, T, G, q_ref, kv_ref, seg_ref, out_ref, buf, stage, qrecv, qt, bias, mx, tot, acc, ostage,
           pre_send, pre_recv, send, recv, out_send, out_recv):
    KR = T
    SR = T + 16
    row = lax.axis_index("row")
    col = lax.axis_index("col")
    z, y = row // Y, row % Y
    x, c = col // 2, col % 2
    o = 1 - c
    me = row * X + x
    C = 2 * T
    W = G * HD
    NX = X - 1
    scale = math.log2(math.e) / math.sqrt(HD)

    def at(zz, yy, xx):
        return (zz * Y + yy, xx * 2 + c)

    sibling = (row, x * 2 + o)
    up = at(z + 1, y, x)
    side = at(z, 1 - y, x)

    def xnext(dx):
        return lax.rem(x + dx, X)

    def xprev(dx):
        return lax.rem(x - dx + X, X)

    barrier = pltpu.get_barrier_semaphore()
    pl.semaphore_signal(barrier, inc=1, device_id=sibling, device_id_type=MESH)
    pl.semaphore_signal(barrier, inc=1, device_id=side, device_id_type=MESH)
    for dx in range(1, X):
        pl.semaphore_signal(barrier, inc=1, device_id=at(z, y, xnext(dx)), device_id_type=MESH)

    @pl.when(z < Z - 1)
    def _():
        pl.semaphore_signal(barrier, inc=1, device_id=up, device_id_type=MESH)

    @pl.when(z > 0)
    def _():
        pl.semaphore_signal(barrier, inc=1, device_id=at(z - 1, y, x), device_id_type=MESH)

    seg16 = jnp.broadcast_to(seg_ref[...].astype(jnp.float32), (16, T)).astype(jnp.bfloat16)

    def piece(ref, h):
        ref[0:KR, :] = kv_ref[:, pl.ds(pl.multiple_of(h * HD, HD), HD)]
        ref[KR:SR, :] = seg16
        ref[SR:, :] = kv_ref[:, pl.ds(pl.multiple_of((KVH + h) * HD, HD), HD)].T

    piece(stage, o)
    pl.semaphore_wait(
        barrier, 2 + NX + jnp.where(z < Z - 1, 1, 0) + jnp.where(z > 0, 1, 0)
    )

    def remote(src, dst, s_sem, r_sem, device):
        return pltpu.make_async_remote_copy(
            src_ref=src, dst_ref=dst, send_sem=s_sem, recv_sem=r_sem, device_id=device, device_id_type=MESH
        )

    kv_swap = remote(stage, buf.at[me, c], pre_send.at[0], pre_recv.at[0], sibling)
    kv_swap.start()
    q_swap = remote(
        q_ref.at[:, pl.ds(pl.multiple_of(o * W, HD), W)], qrecv, pre_send.at[1], pre_recv.at[1], sibling
    )
    q_swap.start()
    piece(buf.at[me, c], c)
    for g in range(G):
        tile = q_ref[:, pl.ds(pl.multiple_of(c * W + g * HD, HD), HD)].T
        qt[0:HD, pl.ds(pl.multiple_of(g * C + c * T, T), T)] = tile
    remote(stage, buf.at[me, o], pre_send.at[0], pre_recv.at[0], sibling).wait_recv()

    def number(zz, yy, xx):
        return (zz * Y + yy) * X + xx

    def copy(kind, s, block, half, device, r_step=None):
        ref = buf.at[block] if half is None else buf.at[block, half]
        return remote(ref, ref, send.at[s, kind], recv.at[s if r_step is None else r_step, kind], device)

    def send_own(s):
        b = number(z - s, y, x)

        @pl.when(s > 0)
        def _():
            copy(0, s, b, None, up).wait_recv()

        @pl.when(z < Z - 1)
        def _():
            copy(0, s, b, None, up, s + 1).start()

        copy(1, s, b, None, side).start()
        for dx in range(1, X):
            copy(1 + dx, s, b, None, at(z, y, xnext(dx))).start()

    def send_diagonal(s):
        b = number(z - s, 1 - y, x)
        copy(1, s, b, None, side).wait_recv()
        for dx in range(1, X):
            copy(1 + NX + dx, s, b, 0, at(z, y, xnext(dx))).start()
        for dx in range(1, X):
            b = number(z - s, y, xprev(dx))
            copy(1 + dx, s, b, None, side).wait_recv()
            copy(1 + 2 * NX + dx, s, b, 1, side).start()

    send_own(jnp.int32(0))

    q_swap.wait_recv()
    for g in range(G):
        qt[0:HD, pl.ds(pl.multiple_of(g * C + o * T, T), T)] = qrecv[:, g * HD:(g + 1) * HD].T
    seg0 = buf[me, 0, KR:SR, :].astype(jnp.float32)
    seg1 = buf[me, 1, KR:SR, :].astype(jnp.float32)
    first = jnp.min(seg0, axis=1, keepdims=True)
    seg_q = jnp.concatenate([seg0, seg1], axis=1)
    hidden = jnp.where(seg_q == first, 0.0, -BIG)
    rows = lax.broadcasted_iota(jnp.int32, (16, C), 0)
    top16 = jnp.where(rows == 0, -BIG, jnp.where(rows == 1, hidden, 0.0)).astype(jnp.bfloat16)
    for g in range(G):
        qt[HD:HD + 16, g * C:(g + 1) * C] = top16
        qt[HD + 16:, g * C:(g + 1) * C] = jnp.zeros((HD - 16, C), jnp.bfloat16)
    turned = [jnp.broadcast_to(s[0:1, :], (T, T)).T for s in (seg0, seg1)]
    seg_k = jnp.concatenate(turned, axis=0)
    seg_k = jnp.concatenate([seg_k, seg_k], axis=1)
    k_at = lax.broadcasted_iota(jnp.int32, (C, C), 0)
    q_at = lax.broadcasted_iota(jnp.int32, (C, C), 1)
    bias[...] = jnp.where((seg_k == seg_q[0:1, :]) & (k_at <= q_at), 0.0, -BIG)

    def values_of(b):
        return jnp.concatenate([buf[b, 0, SR:, :], buf[b, 1, SR:, :]], axis=1)

    keys = jnp.concatenate([buf[me, 0, 0:KR, :], buf[me, 1, 0:KR, :]], axis=0)
    values = values_of(me)
    for g in range(G):
        score = jnp.dot(keys, qt[0:HD, g * C:(g + 1) * C], preferred_element_type=jnp.float32) + bias[...]
        high = jnp.max(score, axis=0, keepdims=True)
        weight = jnp.exp2((score - high) * scale)
        mx[g] = high
        tot[g] = jnp.sum(weight, axis=0, keepdims=True)
        acc[g] = jnp.dot(values, weight.astype(jnp.bfloat16), preferred_element_type=jnp.float32)

    lane = lax.broadcasted_iota(jnp.int32, (T, HD), 1)
    depth = lax.broadcasted_iota(jnp.int32, (T, HD), 0).astype(jnp.float32)

    def half_keys(b, half):
        seg = buf[b, half, KR:SR, :].astype(jnp.float32)
        shown = jnp.sum(jnp.where(seg == first, 1.0, 0.0), axis=1, keepdims=True)
        masked = jnp.where(depth < T - shown[0:1, :], 1.0, 0.0)
        extra = jnp.where(lane == 0, masked, 1.0).astype(jnp.bfloat16)
        return jnp.concatenate([buf[b, half, 0:KR, :], extra], axis=1)

    def attend(b):
        keys = jnp.concatenate([half_keys(b, 0), half_keys(b, 1)], axis=0)
        values = values_of(b)
        for g in range(G):
            score = jnp.dot(keys, qt[:, g * C:(g + 1) * C], preferred_element_type=jnp.float32)
            old = mx[g]
            high = jnp.maximum(old, jnp.max(score, axis=0, keepdims=True))
            weight = jnp.exp2((score - high) * scale)
            factor = jnp.exp2((old - high) * scale)
            mx[g] = high
            tot[g] = tot[g] * factor + jnp.sum(weight, axis=0, keepdims=True)
            acc[g] = acc[g] * factor + jnp.dot(
                values, weight.astype(jnp.bfloat16), preferred_element_type=jnp.float32
            )

    def step(s, unused):
        @pl.when((s > 0) & (s <= z))
        def _():
            send_own(s)

        def early(j, unused):
            p = s - 1
            b = jnp.where(j == 0, number(z - s, y, x), number(z - p, 1 - y, xprev(j)))
            here = jnp.where(j == 0, s <= z, p <= z) & (s > 0)

            @pl.when(here & (j > 0))
            def _():
                copy(1 + NX + j, p, b, 0, side).wait_recv()
                copy(1 + 2 * NX + j, p, b, 1, side).wait_recv()

            @pl.when(here & (b < me))
            def _():
                attend(b)

            return unused

        lax.fori_loop(0, X, early, 0)

        @pl.when(s <= z)
        def _():
            send_diagonal(s)

        def late(j, unused):
            b = jnp.where(j == 0, number(z - s, 1 - y, x), number(z - s, y, xprev(j)))

            @pl.when((s <= z) & (b < me))
            def _():
                attend(b)

            return unused

        lax.fori_loop(0, X, late, 0)
        return unused

    lax.fori_loop(0, Z + 1, step, 0)

    mine = pl.ds(pl.multiple_of(c * T, T), T)
    theirs = pl.ds(pl.multiple_of(o * T, T), T)
    swaps = []
    for g in range(G):
        place = out_ref.at[:, pl.ds(pl.multiple_of(c * W + g * HD, HD), HD)]
        ostage[g] = (acc[g, :, theirs] / tot[g, :, theirs]).T.astype(jnp.bfloat16)
        swap = remote(ostage.at[g], place, out_send.at[g], out_recv.at[g], sibling)
        swap.start()
        swaps.append(swap)
        place[...] = (acc[g, :, mine] / tot[g, :, mine]).T.astype(jnp.bfloat16)

    def drain(s, unused):
        @pl.when(s <= z)
        def _():
            b = number(z - s, y, x)

            @pl.when(z < Z - 1)
            def _():
                copy(0, s, b, None, up, s + 1).wait_send()

            copy(1, s, b, None, side).wait_send()
            for dx in range(1, X):
                copy(1 + dx, s, b, None, side).wait_send()
                copy(1 + NX + dx, s, b, 0, side).wait_send()
                copy(1 + 2 * NX + dx, s, b, 1, side).wait_send()

        return unused

    kv_swap.wait_send()
    q_swap.wait_send()
    lax.fori_loop(0, Z, drain, 0)
    for g in range(G):
        swaps[g].wait_send()
        place = out_ref.at[:, pl.ds(pl.multiple_of(o * W + g * HD, HD), HD)]
        remote(ostage.at[g], place, out_send.at[g], out_recv.at[g], sibling).wait_recv()


def shards(queries, keys_values, segment_ids, n_row, n_col):
    T = queries.shape[0]
    G = queries.shape[1] // (KVH * HD)
    Y = 2
    Z = n_row // Y
    X = n_col // 2
    chips = Z * Y * X
    kinds = 2 + 3 * (X - 1)
    C = 2 * T
    vmem = pl.BlockSpec(memory_space=pltpu.VMEM)
    dma = pltpu.SemaphoreType.DMA
    return pl.pallas_call(
        functools.partial(kernel, Z, Y, X, T, G),
        out_shape=jax.ShapeDtypeStruct(queries.shape, jnp.bfloat16),
        in_specs=[vmem] * 3,
        out_specs=vmem,
        scratch_shapes=[
            pltpu.VMEM((chips, 2, 2 * T + 16, HD), jnp.bfloat16),
            pltpu.VMEM((2 * T + 16, HD), jnp.bfloat16),
            pltpu.VMEM((T, G * HD), jnp.bfloat16),
            pltpu.VMEM((2 * HD, G * C), jnp.bfloat16),
            pltpu.VMEM((C, C), jnp.float32),
            pltpu.VMEM((G, 1, C), jnp.float32),
            pltpu.VMEM((G, 1, C), jnp.float32),
            pltpu.VMEM((G, HD, C), jnp.float32),
            pltpu.VMEM((G, T, HD), jnp.bfloat16),
            dma((2,)),
            dma((2,)),
            dma((Z, kinds)),
            dma((Z, kinds)),
            dma((G,)),
            dma((G,)),
        ],
        compiler_params=pltpu.CompilerParams(
            collective_id=0, has_side_effects=True, vmem_limit_bytes=48 * 1024 * 1024
        ),
    )(queries, keys_values, segment_ids.reshape(1, T))


def solution(mesh):
    in_specs = (P(("row", "col"), None), P(("row", "col"), None), P(("row", "col")))
    out_specs = P(("row", "col"), None)
    body = functools.partial(shards, n_row=mesh.shape["row"], n_col=mesh.shape["col"])
    return jax.shard_map(body, mesh=mesh, in_specs=in_specs, out_specs=out_specs, check_vma=False)
```

profile of v0, /device:TPU:25, one launch (start us, length us, event | category | flops | bytes accessed | tf_op | source)
XLA Modules:
  0.0 46.9 jit_solution(7844932918972843300)
XLA Ops:
  0.0 0.0 copy-start.2
  0.0 0.7 %copy-done.2 = s32[128]{0:T(128)S(1)} copy-done((s32[128]{0:T(128)S(1)}, s32[128]{0:T(128)}, u32[]{:S(2)}) %copy-start.2) | copy-done | bytes 536
  0.7 0.0 copy-start
  0.7 1.0 %copy-done = bf16[128,1792]{1,0:T(8,128)(2,1)S(1)} copy-done((bf16[128,1792]{1,0:T(8,128)(2,1)S(1)}, bf16[128,1792]{1,0:T(8,128)(2,1)}, u32[]{:S(2)}) %copy-start) | copy-done | bytes 458776
  1.7 0.0 copy-start.1
  1.7 0.9 %copy-done.1 = bf16[128,512]{1,0:T(8,128)(2,1)S(1)} copy-done((bf16[128,512]{1,0:T(8,128)(2,1)S(1)}, bf16[128,512]{1,0:T(8,128)(2,1)}, u32[]{:S(2)}) %copy-start.1) | copy-done | bytes 131096
  2.6 43.6 %shard_map.37 = bf16[128,1792]{1,0:T(8,128)(2,1)S(1)} custom-call(bf16[128,1792]{1,0:T(8,128)(2,1)S(1)} %copy-done, bf16[128,512]{1,0:T(8,128)(2,1)S(1)} %copy-done.1, s32[1,128]{1,0:T(1,128)S(1)} %bitcast.1), custom_call_target="tpu_custom_call" | custom-call | tf_op jit(solution)/shard_map/pallas_call | solution.py:269
  46.2 0.8 %copy.5 = bf16[128,1792]{1,0:T(8,128)(2,1)} copy(bf16[128,1792]{1,0:T(8,128)(2,1)S(1)} %shard_map.37) | data formatting | bytes 917504
Async XLA Ops:
  0.0 0.7 %copy-start.2 = (s32[128]{0:T(128)S(1)}, s32[128]{0:T(128)}, u32[]{:S(2)}) copy-start(s32[128]{0:T(128)} %param.5) | copy-start | bytes 1540
  0.7 1.0 %copy-start = (bf16[128,1792]{1,0:T(8,128)(2,1)S(1)}, bf16[128,1792]{1,0:T(8,128)(2,1)}, u32[]{:S(2)}) copy-start(bf16[128,1792]{1,0:T(8,128)(2,1)} %q_ref.1) | copy-start | bytes 1376260
  1.7 0.9 %copy-start.1 = (bf16[128,512]{1,0:T(8,128)(2,1)S(1)}, bf16[128,512]{1,0:T(8,128)(2,1)}, u32[]{:S(2)}) copy-start(bf16[128,512]{1,0:T(8,128)(2,1)} %kv_ref.1) | copy-start | bytes 393220
where the time goes:
time: 47.1 us; the launch traced here: 46.9 us
  Pallas kernels  43.6 us (93%)
  local copies, waits for them, and re-layouts  3.35 us (7%)
    pallas_call x1, Pallas kernels, shards(): pl.pallas_call(functools.partial(kernel, Z, Y, X, T, G), out_shape=jax.Sh...  43.6 us
    unnamed x7, local copies, waits for them, and re-layouts  3.35 us

commit v1 on v0

--- a/solution.py
+++ b/solution.py
@@ -14,7 +14,7 @@
 MESH = pl.DeviceIdType.MESH
 
 
-def kernel(Z, Y, X, T, G, q_ref, kv_ref, seg_ref, out_ref, buf, stage, qrecv, qt, bias, mx, tot, acc, ostage,
+def kernel(Z, Y, X, T, G, q_hbm, kv_hbm, seg_hbm, out_ref, q_ref, kv_ref, seg_ref, load, buf, stage, qrecv, qt, bias, mx, tot, acc, ostage,
            pre_send, pre_recv, send, recv, out_send, out_recv):
     KR = T
     SR = T + 16
@@ -42,6 +42,13 @@
     def xprev(dx):
         return lax.rem(x - dx + X, X)
 
+    q_load = pltpu.make_async_copy(q_hbm.at[:, pl.ds(pl.multiple_of(c * W, HD), W)], q_ref, load.at[0])
+    kv_load = pltpu.make_async_copy(kv_hbm, kv_ref, load.at[1])
+    seg_load = pltpu.make_async_copy(seg_hbm, seg_ref, load.at[2])
+    kv_load.start()
+    seg_load.start()
+    q_load.start()
+
     barrier = pltpu.get_barrier_semaphore()
     pl.semaphore_signal(barrier, inc=1, device_id=sibling, device_id_type=MESH)
     pl.semaphore_signal(barrier, inc=1, device_id=side, device_id_type=MESH)
@@ -56,6 +63,9 @@
     def _():
         pl.semaphore_signal(barrier, inc=1, device_id=at(z - 1, y, x), device_id_type=MESH)
 
+    kv_load.wait()
+    seg_load.wait()
+
     seg16 = jnp.broadcast_to(seg_ref[...].astype(jnp.float32), (16, T)).astype(jnp.bfloat16)
 
     def piece(ref, h):
@@ -76,13 +86,10 @@
     kv_swap = remote(stage, buf.at[me, c], pre_send.at[0], pre_recv.at[0], sibling)
     kv_swap.start()
     q_swap = remote(
-        q_ref.at[:, pl.ds(pl.multiple_of(o * W, HD), W)], qrecv, pre_send.at[1], pre_recv.at[1], sibling
+        q_hbm.at[:, pl.ds(pl.multiple_of(o * W, HD), W)], qrecv, pre_send.at[1], pre_recv.at[1], sibling
     )
     q_swap.start()
     piece(buf.at[me, c], c)
-    for g in range(G):
-        tile = q_ref[:, pl.ds(pl.multiple_of(c * W + g * HD, HD), HD)].T
-        qt[0:HD, pl.ds(pl.multiple_of(g * C + c * T, T), T)] = tile
     remote(stage, buf.at[me, o], pre_send.at[0], pre_recv.at[0], sibling).wait_recv()
 
     def number(zz, yy, xx):
@@ -119,6 +126,9 @@
 
     send_own(jnp.int32(0))
 
+    q_load.wait()
+    for g in range(G):
+        qt[0:HD, pl.ds(pl.multiple_of(g * C + c * T, T), T)] = q_ref[:, g * HD:(g + 1) * HD].T
     q_swap.wait_recv()
     for g in range(G):
         qt[0:HD, pl.ds(pl.multiple_of(g * C + o * T, T), T)] = qrecv[:, g * HD:(g + 1) * HD].T
@@ -182,15 +192,23 @@
         def _():
             send_own(s)
 
-        def early(j, unused):
-            p = s - 1
-            b = jnp.where(j == 0, number(z - s, y, x), number(z - p, 1 - y, xprev(j)))
-            here = jnp.where(j == 0, s <= z, p <= z) & (s > 0)
-
-            @pl.when(here & (j > 0))
+        @pl.when((s > 0) & (s - 1 <= z))
+        def _():
+            send_diagonal(s - 1)
+
+        def blocks(j, unused):
+            dx = jnp.where(j < X, j, j - X)
+            lag = jnp.where(j == 0, 0, jnp.where(j < X, 2, 1))
+            p = s - lag
+            diagonal = (j > 0) & (j < X)
+            yy = jnp.where(diagonal | (j == X), 1 - y, y)
+            b = number(z - p, yy, xprev(dx))
+            here = (p >= jnp.where(j == 0, 1, 0)) & (p <= z)
+
+            @pl.when(here & diagonal)
             def _():
-                copy(1 + NX + j, p, b, 0, side).wait_recv()
-                copy(1 + 2 * NX + j, p, b, 1, side).wait_recv()
+                copy(1 + NX + dx, p, b, 0, side).wait_recv()
+                copy(1 + 2 * NX + dx, p, b, 1, side).wait_recv()
 
             @pl.when(here & (b < me))
             def _():
@@ -198,25 +216,10 @@
 
             return unused
 
-        lax.fori_loop(0, X, early, 0)
-
-        @pl.when(s <= z)
-        def _():
-            send_diagonal(s)
-
-        def late(j, unused):
-            b = jnp.where(j == 0, number(z - s, 1 - y, x), number(z - s, y, xprev(j)))
-
-            @pl.when((s <= z) & (b < me))
-            def _():
-                attend(b)
-
-            return unused
-
-        lax.fori_loop(0, X, late, 0)
+        lax.fori_loop(0, 2 * X, blocks, 0)
         return unused
 
-    lax.fori_loop(0, Z + 1, step, 0)
+    lax.fori_loop(0, Z + 2, step, 0)
 
     mine = pl.ds(pl.multiple_of(c * T, T), T)
     theirs = pl.ds(pl.multiple_of(o * T, T), T)
@@ -269,9 +272,13 @@
     return pl.pallas_call(
         functools.partial(kernel, Z, Y, X, T, G),
         out_shape=jax.ShapeDtypeStruct(queries.shape, jnp.bfloat16),
-        in_specs=[vmem] * 3,
+        in_specs=[pl.BlockSpec(memory_space=pl.ANY)] * 3,
         out_specs=vmem,
         scratch_shapes=[
+            pltpu.VMEM((T, G * HD), jnp.bfloat16),
+            pltpu.VMEM(keys_values.shape, jnp.bfloat16),
+            pltpu.VMEM((1, T), jnp.int32),
+            dma((3,)),
             pltpu.VMEM((chips, 2, 2 * T + 16, HD), jnp.bfloat16),
             pltpu.VMEM((2 * T + 16, HD), jnp.bfloat16),
             pltpu.VMEM((T, G * HD), jnp.bfloat16),
@@ -289,7 +296,7 @@
             dma((G,)),
         ],
         compiler_params=pltpu.CompilerParams(
-            collective_id=0, has_side_effects=True, vmem_limit_bytes=48 * 1024 * 1024
+            collective_id=0, has_side_effects=True, vmem_limit_bytes=60 * 1024 * 1024
         ),
     )(queries, keys_values, segment_ids.reshape(1, T))
 

time: 47.1 us -> 44.9 us (0.953)
  the two profiles are of different devices: /device:TPU:25 before, /device:TPU:31 now
where the time goes in v1:
time: 44.9 us; the launch traced here: 44.7 us
  Pallas kernels  42.9 us (96%)
  local copies, waits for them, and re-layouts  1.82 us (4%)
    pallas_call x1, Pallas kernels, shards(): pl.pallas_call(functools.partial(kernel, Z, Y, X, T, G), out_shape=jax.Sh...  42.9 us
    unnamed x1, local copies, waits for them, and re-layouts  1.82 us

profile of v1, /device:TPU:31, one launch (start us, length us, event | category | flops | bytes accessed | tf_op | source)
XLA Modules:
  0.0 44.7 jit_solution(17062536989104534227)
XLA Ops:
  0.0 42.9 %shard_map.37 = bf16[128,1792]{1,0:T(8,128)(2,1)} custom-call(bf16[128,1792]{1,0:T(8,128)(2,1)} %q_hbm.1, bf16[128,512]{1,0:T(8,128)(2,1)} %kv_hbm.1, s32[1,128]{1,0:T(1,128)} %bitcast.1), custom_call_target="tpu_custom_call" | custom-call | tf_op jit(solution)/shard_map/pallas_call | solution.py:272
  42.9 1.8 %copy.5 = bf16[128,1792]{1,0:T(8,128)(2,1)} copy(bf16[128,1792]{1,0:T(8,128)(2,1)} %shard_map.37) | data formatting | bytes 917504

commit v2 on v1

--- a/solution.py
+++ b/solution.py
@@ -14,7 +14,7 @@
 MESH = pl.DeviceIdType.MESH
 
 
-def kernel(Z, Y, X, T, G, q_hbm, kv_hbm, seg_hbm, out_ref, q_ref, kv_ref, seg_ref, load, buf, stage, qrecv, qt, bias, mx, tot, acc, ostage,
+def kernel(Z, Y, X, T, G, q_hbm, kv_hbm, seg_hbm, out_ref, q_ref, kv_ref, seg_ref, load, buf, stage, qrecv, qt, bias, mx, acc, ostage,
            pre_send, pre_recv, send, recv, out_send, out_recv):
     KR = T
     SR = T + 16
@@ -149,19 +149,6 @@
     q_at = lax.broadcasted_iota(jnp.int32, (C, C), 1)
     bias[...] = jnp.where((seg_k == seg_q[0:1, :]) & (k_at <= q_at), 0.0, -BIG)
 
-    def values_of(b):
-        return jnp.concatenate([buf[b, 0, SR:, :], buf[b, 1, SR:, :]], axis=1)
-
-    keys = jnp.concatenate([buf[me, 0, 0:KR, :], buf[me, 1, 0:KR, :]], axis=0)
-    values = values_of(me)
-    for g in range(G):
-        score = jnp.dot(keys, qt[0:HD, g * C:(g + 1) * C], preferred_element_type=jnp.float32) + bias[...]
-        high = jnp.max(score, axis=0, keepdims=True)
-        weight = jnp.exp2((score - high) * scale)
-        mx[g] = high
-        tot[g] = jnp.sum(weight, axis=0, keepdims=True)
-        acc[g] = jnp.dot(values, weight.astype(jnp.bfloat16), preferred_element_type=jnp.float32)
-
     lane = lax.broadcasted_iota(jnp.int32, (T, HD), 1)
     depth = lax.broadcasted_iota(jnp.int32, (T, HD), 0).astype(jnp.float32)
 
@@ -172,20 +159,49 @@
         extra = jnp.where(lane == 0, masked, 1.0).astype(jnp.bfloat16)
         return jnp.concatenate([buf[b, half, 0:KR, :], extra], axis=1)
 
-    def attend(b):
-        keys = jnp.concatenate([half_keys(b, 0), half_keys(b, 1)], axis=0)
-        values = values_of(b)
+    ones = jnp.ones((16, C), jnp.bfloat16)
+
+    def values_of(b):
+        values = jnp.concatenate([buf[b, 0, SR:, :], buf[b, 1, SR:, :]], axis=1)
+        return jnp.concatenate([values, ones], axis=0)
+
+    def keys_of(b):
+        return jnp.concatenate([half_keys(b, 0), half_keys(b, 1)], axis=0)
+
+    def attend(*blocks):
+        keys = jnp.concatenate([keys_of(b) for b in blocks], axis=0)
+        values = jnp.concatenate([values_of(b) for b in blocks], axis=1)
+
+        def scores(g):
+            return jnp.dot(keys, qt[:, g * C:(g + 1) * C], preferred_element_type=jnp.float32)
+
+        ahead = scores(0)
         for g in range(G):
-            score = jnp.dot(keys, qt[:, g * C:(g + 1) * C], preferred_element_type=jnp.float32)
+            score = ahead
+            if g + 1 < G:
+                ahead = scores(g + 1)
             old = mx[g]
             high = jnp.maximum(old, jnp.max(score, axis=0, keepdims=True))
-            weight = jnp.exp2((score - high) * scale)
+            weight = jnp.exp2((score - high) * scale).astype(jnp.bfloat16)
             factor = jnp.exp2((old - high) * scale)
             mx[g] = high
-            tot[g] = tot[g] * factor + jnp.sum(weight, axis=0, keepdims=True)
-            acc[g] = acc[g] * factor + jnp.dot(
-                values, weight.astype(jnp.bfloat16), preferred_element_type=jnp.float32
-            )
+            acc[g] = acc[g] * factor + jnp.dot(values, weight, preferred_element_type=jnp.float32)
+
+    keys = jnp.concatenate([buf[me, 0, 0:KR, :], buf[me, 1, 0:KR, :]], axis=0)
+    values = values_of(me)
+
+    def own_scores(g):
+        return jnp.dot(keys, qt[0:HD, g * C:(g + 1) * C], preferred_element_type=jnp.float32)
+
+    ahead = own_scores(0)
+    for g in range(G):
+        score = ahead + bias[...]
+        if g + 1 < G:
+            ahead = own_scores(g + 1)
+        high = jnp.max(score, axis=0, keepdims=True)
+        weight = jnp.exp2((score - high) * scale).astype(jnp.bfloat16)
+        mx[g] = high
+        acc[g] = jnp.dot(values, weight, preferred_element_type=jnp.float32)
 
     def step(s, unused):
         @pl.when((s > 0) & (s <= z))
@@ -196,10 +212,9 @@
         def _():
             send_diagonal(s - 1)
 
-        def blocks(j, unused):
+        def entry(j):
             dx = jnp.where(j < X, j, j - X)
-            lag = jnp.where(j == 0, 0, jnp.where(j < X, 2, 1))
-            p = s - lag
+            p = s - jnp.where(j == 0, 0, jnp.where(j < X, 2, 1))
             diagonal = (j > 0) & (j < X)
             yy = jnp.where(diagonal | (j == X), 1 - y, y)
             b = number(z - p, yy, xprev(dx))
@@ -210,13 +225,23 @@
                 copy(1 + NX + dx, p, b, 0, side).wait_recv()
                 copy(1 + 2 * NX + dx, p, b, 1, side).wait_recv()
 
-            @pl.when(here & (b < me))
+            return b, here & (b < me)
+
+        def blocks(j, unused):
+            b0, shown0 = entry(2 * j)
+            b1, shown1 = entry(2 * j + 1)
+
+            @pl.when(shown0 & shown1)
             def _():
-                attend(b)
+                attend(b0, b1)
+
+            @pl.when(shown0 != shown1)
+            def _():
+                attend(jnp.where(shown0, b0, b1))
 
             return unused
 
-        lax.fori_loop(0, 2 * X, blocks, 0)
+        lax.fori_loop(0, X, blocks, 0)
         return unused
 
     lax.fori_loop(0, Z + 2, step, 0)
@@ -226,11 +251,11 @@
     swaps = []
     for g in range(G):
         place = out_ref.at[:, pl.ds(pl.multiple_of(c * W + g * HD, HD), HD)]
-        ostage[g] = (acc[g, :, theirs] / tot[g, :, theirs]).T.astype(jnp.bfloat16)
+        ostage[g] = (acc[g, 0:HD, theirs] / acc[g, HD:HD + 1, theirs]).astype(jnp.bfloat16).T
         swap = remote(ostage.at[g], place, out_send.at[g], out_recv.at[g], sibling)
         swap.start()
         swaps.append(swap)
-        place[...] = (acc[g, :, mine] / tot[g, :, mine]).T.astype(jnp.bfloat16)
+        place[...] = (acc[g, 0:HD, mine] / acc[g, HD:HD + 1, mine]).astype(jnp.bfloat16).T
 
     def drain(s, unused):
         @pl.when(s <= z)
@@ -285,8 +310,7 @@
             pltpu.VMEM((2 * HD, G * C), jnp.bfloat16),
             pltpu.VMEM((C, C), jnp.float32),
             pltpu.VMEM((G, 1, C), jnp.float32),
-            pltpu.VMEM((G, 1, C), jnp.float32),
-            pltpu.VMEM((G, HD, C), jnp.float32),
+            pltpu.VMEM((G, HD + 16, C), jnp.float32),
             pltpu.VMEM((G, T, HD), jnp.bfloat16),
             dma((2,)),
             dma((2,)),

time: 44.9 us -> 33 us (0.73)
  the two profiles are of different devices: /device:TPU:31 before, /device:TPU:25 now
where the time goes in v2:
time: 33 us; the launch traced here: 32.9 us
  Pallas kernels  31 us (94%)
  local copies, waits for them, and re-layouts  1.82 us (6%)
    pallas_call x1, Pallas kernels, shards(): pl.pallas_call(functools.partial(kernel, Z, Y, X, T, G), out_shape=jax.Sh...  31 us
    unnamed x1, local copies, waits for them, and re-layouts  1.82 us

profile of v2, /device:TPU:25, one launch (start us, length us, event | category | flops | bytes accessed | tf_op | source)
XLA Modules:
  0.0 32.9 jit_solution(14163002558241511765)
XLA Ops:
  0.0 31.0 %shard_map.37 = bf16[128,1792]{1,0:T(8,128)(2,1)} custom-call(bf16[128,1792]{1,0:T(8,128)(2,1)} %q_hbm.1, bf16[128,512]{1,0:T(8,128)(2,1)} %kv_hbm.1, s32[1,128]{1,0:T(1,128)} %bitcast.1), custom_call_target="tpu_custom_call" | custom-call | tf_op jit(solution)/shard_map/pallas_call | solution.py:297
  31.0 1.8 %copy.5 = bf16[128,1792]{1,0:T(8,128)(2,1)} copy(bf16[128,1792]{1,0:T(8,128)(2,1)} %shard_map.37) | data formatting | bytes 917504

commit v3 on v2

--- a/solution.py
+++ b/solution.py
@@ -27,6 +27,7 @@
     C = 2 * T
     W = G * HD
     NX = X - 1
+    reach = 3 * (Z * Y * X) // 4
     scale = math.log2(math.e) / math.sqrt(HD)
 
     def at(zz, yy, xx):
@@ -99,30 +100,62 @@
         ref = buf.at[block] if half is None else buf.at[block, half]
         return remote(ref, ref, send.at[s, kind], recv.at[s if r_step is None else r_step, kind], device)
 
+    def need(b, zz, yy, xx):
+        i = number(zz, yy, xx)
+        return (b < i) & (b >= i - reach)
+
+    def for_row(b, yy):
+        start = number(z, yy, 0)
+        return (b < start + X - 1) & (b >= start - reach)
+
+    def for_column(b, xx):
+        return need(b, z, 0, xx) | need(b, z, 1, xx)
+
+    def for_plane(b, zz):
+        return b >= zz * Y * X - reach
+
     def send_own(s):
         b = number(z - s, y, x)
 
-        @pl.when(s > 0)
+        @pl.when((s > 0) & for_plane(b, z))
         def _():
             copy(0, s, b, None, up).wait_recv()
 
-        @pl.when(z < Z - 1)
+        @pl.when((z < Z - 1) & for_plane(b, z + 1))
         def _():
             copy(0, s, b, None, up, s + 1).start()
 
-        copy(1, s, b, None, side).start()
+        @pl.when(for_row(b, 1 - y))
+        def _():
+            copy(1, s, b, None, side).start()
+
         for dx in range(1, X):
-            copy(1 + dx, s, b, None, at(z, y, xnext(dx))).start()
+            @pl.when(for_column(b, xnext(dx)))
+            def _():
+                copy(1 + dx, s, b, None, at(z, y, xnext(dx))).start()
 
     def send_diagonal(s):
         b = number(z - s, 1 - y, x)
-        copy(1, s, b, None, side).wait_recv()
+
+        @pl.when(for_row(b, y))
+        def _():
+            copy(1, s, b, None, side).wait_recv()
+
         for dx in range(1, X):
-            copy(1 + NX + dx, s, b, 0, at(z, y, xnext(dx))).start()
+            @pl.when(need(b, z, y, xnext(dx)))
+            def _():
+                copy(1 + NX + dx, s, b, 0, at(z, y, xnext(dx))).start()
+
         for dx in range(1, X):
-            b = number(z - s, y, xprev(dx))
-            copy(1 + dx, s, b, None, side).wait_recv()
-            copy(1 + 2 * NX + dx, s, b, 1, side).start()
+            e = number(z - s, y, xprev(dx))
+
+            @pl.when(for_column(e, x))
+            def _():
+                copy(1 + dx, s, e, None, side).wait_recv()
+
+            @pl.when(need(e, z, 1 - y, x))
+            def _():
+                copy(1 + 2 * NX + dx, s, e, 1, side).start()
 
     send_own(jnp.int32(0))
 
@@ -218,14 +251,14 @@
             diagonal = (j > 0) & (j < X)
             yy = jnp.where(diagonal | (j == X), 1 - y, y)
             b = number(z - p, yy, xprev(dx))
-            here = (p >= jnp.where(j == 0, 1, 0)) & (p <= z)
+            here = (p >= jnp.where(j == 0, 1, 0)) & (p <= z) & need(b, z, y, x)
 
             @pl.when(here & diagonal)
             def _():
                 copy(1 + NX + dx, p, b, 0, side).wait_recv()
                 copy(1 + 2 * NX + dx, p, b, 1, side).wait_recv()
 
-            return b, here & (b < me)
+            return b, here
 
         def blocks(j, unused):
             b0, shown0 = entry(2 * j)
@@ -262,15 +295,29 @@
         def _():
             b = number(z - s, y, x)
 
-            @pl.when(z < Z - 1)
+            @pl.when((z < Z - 1) & for_plane(b, z + 1))
             def _():
                 copy(0, s, b, None, up, s + 1).wait_send()
 
-            copy(1, s, b, None, side).wait_send()
+            @pl.when(for_row(b, 1 - y))
+            def _():
+                copy(1, s, b, None, side).wait_send()
+
             for dx in range(1, X):
-                copy(1 + dx, s, b, None, side).wait_send()
-                copy(1 + NX + dx, s, b, 0, side).wait_send()
-                copy(1 + 2 * NX + dx, s, b, 1, side).wait_send()
+                d = number(z - s, 1 - y, x)
+                e = number(z - s, y, xprev(dx))
+
+                @pl.when(for_column(b, xnext(dx)))
+                def _():
+                    copy(1 + dx, s, b, None, side).wait_send()
+
+                @pl.when(need(d, z, y, xnext(dx)))
+                def _():
+                    copy(1 + NX + dx, s, d, 0, side).wait_send()
+
+                @pl.when(need(e, z, 1 - y, x))
+                def _():
+                    copy(1 + 2 * NX + dx, s, e, 1, side).wait_send()
 
         return unused
 

time: 33 us -> 33.1 us (level)
  no operation moved by 1% of the time
where the time goes in v3:
time: 33.1 us; the launch traced here: 32.9 us
  Pallas kernels  31.1 us (94%)
  local copies, waits for them, and re-layouts  1.82 us (5%)
    pallas_call x1, Pallas kernels, shards(): pl.pallas_call(functools.partial(kernel, Z, Y, X, T, G), out_shape=jax.Sh...  31.1 us
    unnamed x1, local copies, waits for them, and re-layouts  1.82 us

profile of v3, /device:TPU:25, one launch (start us, length us, event | category | flops | bytes accessed | tf_op | source)
XLA Modules:
  0.0 32.9 jit_solution(4125692534038598608)
XLA Ops:
  0.0 31.1 %shard_map.37 = bf16[128,1792]{1,0:T(8,128)(2,1)} custom-call(bf16[128,1792]{1,0:T(8,128)(2,1)} %q_hbm.1, bf16[128,512]{1,0:T(8,128)(2,1)} %kv_hbm.1, s32[1,128]{1,0:T(1,128)} %bitcast.1), custom_call_target="tpu_custom_call" | custom-call | tf_op jit(solution)/shard_map/pallas_call | solution.py:344
  31.1 1.8 %copy.5 = bf16[128,1792]{1,0:T(8,128)(2,1)} copy(bf16[128,1792]{1,0:T(8,128)(2,1)} %shard_map.37) | data formatting | bytes 917504

commit v4 on v3

--- a/solution.py
+++ b/solution.py
@@ -14,7 +14,7 @@
 MESH = pl.DeviceIdType.MESH
 
 
-def kernel(Z, Y, X, T, G, q_hbm, kv_hbm, seg_hbm, out_ref, q_ref, kv_ref, seg_ref, load, buf, stage, qrecv, qt, bias, mx, acc, ostage,
+def kernel(Z, Y, X, T, G, q_hbm, kv_ref, seg_ref, out_ref, q_ref, load, buf, stage, qrecv, qt, bias, mx, acc, ostage,
            pre_send, pre_recv, send, recv, out_send, out_recv):
     KR = T
     SR = T + 16
@@ -43,11 +43,7 @@
     def xprev(dx):
         return lax.rem(x - dx + X, X)
 
-    q_load = pltpu.make_async_copy(q_hbm.at[:, pl.ds(pl.multiple_of(c * W, HD), W)], q_ref, load.at[0])
-    kv_load = pltpu.make_async_copy(kv_hbm, kv_ref, load.at[1])
-    seg_load = pltpu.make_async_copy(seg_hbm, seg_ref, load.at[2])
-    kv_load.start()
-    seg_load.start()
+    q_load = pltpu.make_async_copy(q_hbm.at[:, pl.ds(pl.multiple_of(c * W, HD), W)], q_ref, load)
     q_load.start()
 
     barrier = pltpu.get_barrier_semaphore()
@@ -63,9 +59,6 @@
     @pl.when(z > 0)
     def _():
         pl.semaphore_signal(barrier, inc=1, device_id=at(z - 1, y, x), device_id_type=MESH)
-
-    kv_load.wait()
-    seg_load.wait()
 
     seg16 = jnp.broadcast_to(seg_ref[...].astype(jnp.float32), (16, T)).astype(jnp.bfloat16)
 
@@ -91,77 +84,98 @@
     )
     q_swap.start()
     piece(buf.at[me, c], c)
-    remote(stage, buf.at[me, o], pre_send.at[0], pre_recv.at[0], sibling).wait_recv()
 
     def number(zz, yy, xx):
         return (zz * Y + yy) * X + xx
 
+    def along_x(dx, half):
+        return 2 + 2 * dx + half
+
+    def onward_x(dx):
+        return 3 + 2 * NX + dx
+
+    def onward_y(dx):
+        return 3 + 3 * NX + dx
+
     def copy(kind, s, block, half, device, r_step=None):
-        ref = buf.at[block] if half is None else buf.at[block, half]
+        ref = buf.at[block, half]
         return remote(ref, ref, send.at[s, kind], recv.at[s if r_step is None else r_step, kind], device)
 
     def need(b, zz, yy, xx):
         i = number(zz, yy, xx)
         return (b < i) & (b >= i - reach)
 
-    def for_row(b, yy):
+    def for_row(b, yy, half):
         start = number(z, yy, 0)
-        return (b < start + X - 1) & (b >= start - reach)
-
-    def for_column(b, xx):
-        return need(b, z, 0, xx) | need(b, z, 1, xx)
+        return jnp.where(half == 0, (b < start + X - 1) & (b >= start - reach), need(b, z, yy, x))
+
+    def for_column(b, xx, half):
+        return need(b, z, y, xx) | (need(b, z, 1 - y, xx) & (half == 1))
 
     def for_plane(b, zz):
         return b >= zz * Y * X - reach
 
-    def send_own(s):
+    def send_half(s, half):
         b = number(z - s, y, x)
 
         @pl.when((s > 0) & for_plane(b, z))
         def _():
-            copy(0, s, b, None, up).wait_recv()
+            copy(half, s, b, half, up).wait_recv()
 
         @pl.when((z < Z - 1) & for_plane(b, z + 1))
         def _():
-            copy(0, s, b, None, up, s + 1).start()
-
-        @pl.when(for_row(b, 1 - y))
-        def _():
-            copy(1, s, b, None, side).start()
+            copy(half, s, b, half, up, s + 1).start()
+
+        @pl.when(for_row(b, 1 - y, half))
+        def _():
+            copy(2 + half, s, b, half, side).start()
 
         for dx in range(1, X):
-            @pl.when(for_column(b, xnext(dx)))
-            def _():
-                copy(1 + dx, s, b, None, at(z, y, xnext(dx))).start()
+            @pl.when(for_column(b, xnext(dx), half))
+            def _():
+                copy(along_x(dx, half), s, b, half, at(z, y, xnext(dx))).start()
 
     def send_diagonal(s):
         b = number(z - s, 1 - y, x)
 
-        @pl.when(for_row(b, y))
-        def _():
-            copy(1, s, b, None, side).wait_recv()
+        @pl.when(for_row(b, y, 0))
+        def _():
+            copy(2, s, b, 0, side).wait_recv()
 
         for dx in range(1, X):
             @pl.when(need(b, z, y, xnext(dx)))
             def _():
-                copy(1 + NX + dx, s, b, 0, at(z, y, xnext(dx))).start()
+                copy(onward_x(dx), s, b, 0, at(z, y, xnext(dx))).start()
 
         for dx in range(1, X):
             e = number(z - s, y, xprev(dx))
 
-            @pl.when(for_column(e, x))
-            def _():
-                copy(1 + dx, s, e, None, side).wait_recv()
+            @pl.when(for_column(e, x, 1))
+            def _():
+                copy(along_x(dx, 1), s, e, 1, side).wait_recv()
 
             @pl.when(need(e, z, 1 - y, x))
             def _():
-                copy(1 + 2 * NX + dx, s, e, 1, side).start()
-
-    send_own(jnp.int32(0))
-
+                copy(onward_y(dx), s, e, 1, side).start()
+
+    def relay(s):
+        @pl.when(s <= z)
+        def _():
+            send_half(s, 0)
+            send_half(s, 1)
+
+        @pl.when(s - 1 <= z)
+        def _():
+            send_diagonal(s - 1)
+
+    start = jnp.int32(0)
+    send_half(start, c)
     q_load.wait()
     for g in range(G):
         qt[0:HD, pl.ds(pl.multiple_of(g * C + c * T, T), T)] = q_ref[:, g * HD:(g + 1) * HD].T
+    remote(stage, buf.at[me, o], pre_send.at[0], pre_recv.at[0], sibling).wait_recv()
+    send_half(start, o)
+
     q_swap.wait_recv()
     for g in range(G):
         qt[0:HD, pl.ds(pl.multiple_of(g * C + o * T, T), T)] = qrecv[:, g * HD:(g + 1) * HD].T
@@ -220,6 +234,8 @@
             mx[g] = high
             acc[g] = acc[g] * factor + jnp.dot(values, weight, preferred_element_type=jnp.float32)
 
+    relay(jnp.int32(1))
+
     keys = jnp.concatenate([buf[me, 0, 0:KR, :], buf[me, 1, 0:KR, :]], axis=0)
     values = values_of(me)
 
@@ -237,13 +253,9 @@
         acc[g] = jnp.dot(values, weight, preferred_element_type=jnp.float32)
 
     def step(s, unused):
-        @pl.when((s > 0) & (s <= z))
-        def _():
-            send_own(s)
-
-        @pl.when((s > 0) & (s - 1 <= z))
-        def _():
-            send_diagonal(s - 1)
+        @pl.when(s > 1)
+        def _():
+            relay(s)
 
         def entry(j):
             dx = jnp.where(j < X, j, j - X)
@@ -255,8 +267,16 @@
 
             @pl.when(here & diagonal)
             def _():
-                copy(1 + NX + dx, p, b, 0, side).wait_recv()
-                copy(1 + 2 * NX + dx, p, b, 1, side).wait_recv()
+                copy(onward_x(dx), p, b, 0, side).wait_recv()
+                copy(onward_y(dx), p, b, 1, side).wait_recv()
+
+            @pl.when(here & (j == X))
+            def _():
+                copy(3, p, b, 1, side).wait_recv()
+
+            @pl.when(here & (j > X))
+            def _():
+                copy(along_x(dx, 0), p, b, 0, side).wait_recv()
 
             return b, here
 
@@ -277,7 +297,7 @@
         lax.fori_loop(0, X, blocks, 0)
         return unused
 
-    lax.fori_loop(0, Z + 2, step, 0)
+    lax.fori_loop(1, Z + 2, step, 0)
 
     mine = pl.ds(pl.multiple_of(c * T, T), T)
     theirs = pl.ds(pl.multiple_of(o * T, T), T)
@@ -295,29 +315,31 @@
         def _():
             b = number(z - s, y, x)
 
-            @pl.when((z < Z - 1) & for_plane(b, z + 1))
-            def _():
-                copy(0, s, b, None, up, s + 1).wait_send()
-
-            @pl.when(for_row(b, 1 - y))
-            def _():
-                copy(1, s, b, None, side).wait_send()
+            for half in range(2):
+                @pl.when((z < Z - 1) & for_plane(b, z + 1))
+                def _():
+                    copy(half, s, b, half, up, s + 1).wait_send()
+
+                @pl.when(for_row(b, 1 - y, half))
+                def _():
+                    copy(2 + half, s, b, half, side).wait_send()
+
+                for dx in range(1, X):
+                    @pl.when(for_column(b, xnext(dx), half))
+                    def _():
+                        copy(along_x(dx, half), s, b, half, side).wait_send()
 
             for dx in range(1, X):
                 d = number(z - s, 1 - y, x)
                 e = number(z - s, y, xprev(dx))
 
-                @pl.when(for_column(b, xnext(dx)))
-                def _():
-                    copy(1 + dx, s, b, None, side).wait_send()
-
                 @pl.when(need(d, z, y, xnext(dx)))
                 def _():
-                    copy(1 + NX + dx, s, d, 0, side).wait_send()
+                    copy(onward_x(dx), s, d, 0, side).wait_send()
 
                 @pl.when(need(e, z, 1 - y, x))
                 def _():
-                    copy(1 + 2 * NX + dx, s, e, 1, side).wait_send()
+                    copy(onward_y(dx), s, e, 1, side).wait_send()
 
         return unused
 
@@ -337,20 +359,18 @@
     Z = n_row // Y
     X = n_col // 2
     chips = Z * Y * X
-    kinds = 2 + 3 * (X - 1)
+    kinds = 4 + 4 * (X - 1)
     C = 2 * T
     vmem = pl.BlockSpec(memory_space=pltpu.VMEM)
     dma = pltpu.SemaphoreType.DMA
     return pl.pallas_call(
         functools.partial(kernel, Z, Y, X, T, G),
         out_shape=jax.ShapeDtypeStruct(queries.shape, jnp.bfloat16),
-        in_specs=[pl.BlockSpec(memory_space=pl.ANY)] * 3,
+        in_specs=[pl.BlockSpec(memory_space=pl.ANY), vmem, vmem],
         out_specs=vmem,
         scratch_shapes=[
             pltpu.VMEM((T, G * HD), jnp.bfloat16),
-            pltpu.VMEM(keys_values.shape, jnp.bfloat16),
-            pltpu.VMEM((1, T), jnp.int32),
-            dma((3,)),
+            dma,
             pltpu.VMEM((chips, 2, 2 * T + 16, HD), jnp.bfloat16),
             pltpu.VMEM((2 * T + 16, HD), jnp.bfloat16),
             pltpu.VMEM((T, G * HD), jnp.bfloat16),
@@ -367,7 +387,7 @@
             dma((G,)),
         ],
         compiler_params=pltpu.CompilerParams(
-            collective_id=0, has_side_effects=True, vmem_limit_bytes=60 * 1024 * 1024
+            collective_id=0, has_side_effects=True, vmem_limit_bytes=53 * 1024 * 1024
         ),
     )(queries, keys_values, segment_ids.reshape(1, T))
 

time: 33.1 us -> 32.2 us (0.973)
  Pallas kernels: 31.1 us -> 29.7 us
  local copies, waits for them, and re-layouts: 1.82 us -> 2.33 us
    pallas_call x1, Pallas kernels: 31.1 us -> 29.7 us  [shards(): pl.pallas_call(functools.partial(kernel, Z, Y, X, T, G), out_shape=jax.Sh...]
    unnamed x1 -> x5, local copies, waits for them, and re-layouts: 1.82 us -> 2.33 us
where the time goes in v4:
time: 32.2 us; the launch traced here: 32.1 us
  Pallas kernels  29.7 us (92%)
  local copies, waits for them, and re-layouts  2.33 us (7%)
    pallas_call x1, Pallas kernels, shards(): pl.pallas_call(functools.partial(kernel, Z, Y, X, T, G), out_shape=jax.Sh...  29.7 us
    unnamed x5, local copies, waits for them, and re-layouts  2.33 us

profile of v4, /device:TPU:25, one launch (start us, length us, event | category | flops | bytes accessed | tf_op | source)
XLA Modules:
  0.0 32.1 jit_solution(40898696645355206)
XLA Ops:
  0.0 0.0 copy-start.1
  0.0 0.7 %copy-done.1 = s32[128]{0:T(128)S(1)} copy-done((s32[128]{0:T(128)S(1)}, s32[128]{0:T(128)}, u32[]{:S(2)}) %copy-start.1) | copy-done | bytes 536
  0.7 0.0 copy-start
  0.7 0.9 %copy-done = bf16[128,512]{1,0:T(8,128)(2,1)S(1)} copy-done((bf16[128,512]{1,0:T(8,128)(2,1)S(1)}, bf16[128,512]{1,0:T(8,128)(2,1)}, u32[]{:S(2)}) %copy-start) | copy-done | bytes 131096
  1.6 29.7 %shard_map.37 = bf16[128,1792]{1,0:T(8,128)(2,1)S(1)} custom-call(bf16[128,1792]{1,0:T(8,128)(2,1)} %q_hbm.1, bf16[128,512]{1,0:T(8,128)(2,1)S(1)} %copy-done, s32[1,128]{1,0:T(1,128)S(1)} %bitcast.1), custom_call_target="tpu_custom_call" | custom-call | tf_op jit(solution)/shard_map/pallas_call | solution.py:366
  31.3 0.8 %copy.5 = bf16[128,1792]{1,0:T(8,128)(2,1)} copy(bf16[128,1792]{1,0:T(8,128)(2,1)S(1)} %shard_map.37) | data formatting | bytes 917504
Async XLA Ops:
  0.0 0.7 %copy-start.1 = (s32[128]{0:T(128)S(1)}, s32[128]{0:T(128)}, u32[]{:S(2)}) copy-start(s32[128]{0:T(128)} %param.5) | copy-start | bytes 1540
  0.7 0.9 %copy-start = (bf16[128,512]{1,0:T(8,128)(2,1)S(1)}, bf16[128,512]{1,0:T(8,128)(2,1)}, u32[]{:S(2)}) copy-start(bf16[128,512]{1,0:T(8,128)(2,1)} %kv_ref.1) | copy-start | bytes 393220

commit v5 on v4

--- a/solution.py
+++ b/solution.py
@@ -222,17 +222,24 @@
         def scores(g):
             return jnp.dot(keys, qt[:, g * C:(g + 1) * C], preferred_element_type=jnp.float32)
 
+        def finish(g, factor, weight):
+            acc[g] = acc[g] * factor + jnp.dot(values, weight, preferred_element_type=jnp.float32)
+
         ahead = scores(0)
+        behind = None
         for g in range(G):
             score = ahead
             if g + 1 < G:
                 ahead = scores(g + 1)
             old = mx[g]
             high = jnp.maximum(old, jnp.max(score, axis=0, keepdims=True))
-            weight = jnp.exp2((score - high) * scale).astype(jnp.bfloat16)
+            weight = jnp.exp2(((score - high) * scale).astype(jnp.bfloat16))
             factor = jnp.exp2((old - high) * scale)
             mx[g] = high
-            acc[g] = acc[g] * factor + jnp.dot(values, weight, preferred_element_type=jnp.float32)
+            if behind is not None:
+                finish(*behind)
+            behind = (g, factor, weight)
+        finish(*behind)
 
     relay(jnp.int32(1))
 
@@ -248,7 +255,7 @@
         if g + 1 < G:
             ahead = own_scores(g + 1)
         high = jnp.max(score, axis=0, keepdims=True)
-        weight = jnp.exp2((score - high) * scale).astype(jnp.bfloat16)
+        weight = jnp.exp2(((score - high) * scale).astype(jnp.bfloat16))
         mx[g] = high
         acc[g] = jnp.dot(values, weight, preferred_element_type=jnp.float32)
 

time: 32.2 us -> 32.4 us (level)
  no operation moved by 1% of the time
where the time goes in v5:
time: 32.4 us; the launch traced here: 32.2 us
  Pallas kernels  29.9 us (92%)
  local copies, waits for them, and re-layouts  2.33 us (7%)
    pallas_call x1, Pallas kernels, shards(): pl.pallas_call(functools.partial(kernel, Z, Y, X, T, G), out_shape=jax.Sh...  29.9 us
    unnamed x5, local copies, waits for them, and re-layouts  2.33 us

profile of v5, /device:TPU:25, one launch (start us, length us, event | category | flops | bytes accessed | tf_op | source)
XLA Modules:
  0.0 32.2 jit_solution(4528287246626311411)
XLA Ops:
  0.0 0.0 copy-start.1
  0.0 0.7 %copy-done.1 = s32[128]{0:T(128)S(1)} copy-done((s32[128]{0:T(128)S(1)}, s32[128]{0:T(128)}, u32[]{:S(2)}) %copy-start.1) | copy-done | bytes 536
  0.7 0.0 copy-start
  0.7 0.9 %copy-done = bf16[128,512]{1,0:T(8,128)(2,1)S(1)} copy-done((bf16[128,512]{1,0:T(8,128)(2,1)S(1)}, bf16[128,512]{1,0:T(8,128)(2,1)}, u32[]{:S(2)}) %copy-start) | copy-done | bytes 131096
  1.6 29.9 %shard_map.37 = bf16[128,1792]{1,0:T(8,128)(2,1)S(1)} custom-call(bf16[128,1792]{1,0:T(8,128)(2,1)} %q_hbm.1, bf16[128,512]{1,0:T(8,128)(2,1)S(1)} %copy-done, s32[1,128]{1,0:T(1,128)S(1)} %bitcast.1), custom_call_target="tpu_custom_call" | custom-call | tf_op jit(solution)/shard_map/pallas_call | solution.py:373
  31.5 0.8 %copy.5 = bf16[128,1792]{1,0:T(8,128)(2,1)} copy(bf16[128,1792]{1,0:T(8,128)(2,1)S(1)} %shard_map.37) | data formatting | bytes 917504
Async XLA Ops:
  0.0 0.7 %copy-start.1 = (s32[128]{0:T(128)S(1)}, s32[128]{0:T(128)}, u32[]{:S(2)}) copy-start(s32[128]{0:T(128)} %param.5) | copy-start | bytes 1540
  0.7 0.9 %copy-start = (bf16[128,512]{1,0:T(8,128)(2,1)S(1)}, bf16[128,512]{1,0:T(8,128)(2,1)}, u32[]{:S(2)}) copy-start(bf16[128,512]{1,0:T(8,128)(2,1)} %kv_ref.1) | copy-start | bytes 393220

commit v6 on v5

--- a/solution.py
+++ b/solution.py
@@ -158,15 +158,16 @@
             def _():
                 copy(onward_y(dx), s, e, 1, side).start()
 
-    def relay(s):
+    def pass_up(s):
         @pl.when(s <= z)
         def _():
             send_half(s, 0)
             send_half(s, 1)
 
-        @pl.when(s - 1 <= z)
-        def _():
-            send_diagonal(s - 1)
+    def pass_on(s):
+        @pl.when(s <= z)
+        def _():
+            send_diagonal(s)
 
     start = jnp.int32(0)
     send_half(start, c)
@@ -241,7 +242,8 @@
             behind = (g, factor, weight)
         finish(*behind)
 
-    relay(jnp.int32(1))
+    pass_up(jnp.int32(1))
+    pass_on(start)
 
     keys = jnp.concatenate([buf[me, 0, 0:KR, :], buf[me, 1, 0:KR, :]], axis=0)
     values = values_of(me)
@@ -260,34 +262,36 @@
         acc[g] = jnp.dot(values, weight, preferred_element_type=jnp.float32)
 
     def step(s, unused):
-        @pl.when(s > 1)
-        def _():
-            relay(s)
+        pass_up(s + 1)
 
         def entry(j):
-            dx = jnp.where(j < X, j, j - X)
-            p = s - jnp.where(j == 0, 0, jnp.where(j < X, 2, 1))
-            diagonal = (j > 0) & (j < X)
-            yy = jnp.where(diagonal | (j == X), 1 - y, y)
+            dx = lax.rem(j, X)
+            p = jnp.where(j == X, s, s - 1)
+            diagonal = j > X
+            yy = jnp.where(diagonal | (j == 0), 1 - y, y)
             b = number(z - p, yy, xprev(dx))
-            here = (p >= jnp.where(j == 0, 1, 0)) & (p <= z) & need(b, z, y, x)
+            here = (p <= z) & need(b, z, y, x)
 
             @pl.when(here & diagonal)
             def _():
                 copy(onward_x(dx), p, b, 0, side).wait_recv()
                 copy(onward_y(dx), p, b, 1, side).wait_recv()
 
-            @pl.when(here & (j == X))
+            @pl.when(here & (j == 0))
             def _():
                 copy(3, p, b, 1, side).wait_recv()
 
-            @pl.when(here & (j > X))
+            @pl.when(here & (j > 0) & (j < X))
             def _():
                 copy(along_x(dx, 0), p, b, 0, side).wait_recv()
 
             return b, here
 
         def blocks(j, unused):
+            @pl.when(j == X // 2)
+            def _():
+                pass_on(s)
+
             b0, shown0 = entry(2 * j)
             b1, shown1 = entry(2 * j + 1)
 
@@ -304,7 +308,7 @@
         lax.fori_loop(0, X, blocks, 0)
         return unused
 
-    lax.fori_loop(1, Z + 2, step, 0)
+    lax.fori_loop(1, Z + 1, step, 0)
 
     mine = pl.ds(pl.multiple_of(c * T, T), T)
     theirs = pl.ds(pl.multiple_of(o * T, T), T)

time: 32.4 us -> 31.1 us (0.960)
  Pallas kernels: 29.9 us -> 28.6 us
    pallas_call x1, Pallas kernels: 29.9 us -> 28.6 us  [shards(): pl.pallas_call(functools.partial(kernel, Z, Y, X, T, G), out_shape=jax.Sh...]
where the time goes in v6:
time: 31.1 us; the launch traced here: 31 us
  Pallas kernels  28.6 us (92%)
  local copies, waits for them, and re-layouts  2.33 us (7%)
    pallas_call x1, Pallas kernels, shards(): pl.pallas_call(functools.partial(kernel, Z, Y, X, T, G), out_shape=jax.Sh...  28.6 us
    unnamed x5, local copies, waits for them, and re-layouts  2.33 us

profile of v6, /device:TPU:25, one launch (start us, length us, event | category | flops | bytes accessed | tf_op | source)
XLA Modules:
  0.0 31.0 jit_solution(10679533660936179050)
XLA Ops:
  0.0 0.0 copy-start.1
  0.0 0.7 %copy-done.1 = s32[128]{0:T(128)S(1)} copy-done((s32[128]{0:T(128)S(1)}, s32[128]{0:T(128)}, u32[]{:S(2)}) %copy-start.1) | copy-done | bytes 536
  0.7 0.0 copy-start
  0.7 0.9 %copy-done = bf16[128,512]{1,0:T(8,128)(2,1)S(1)} copy-done((bf16[128,512]{1,0:T(8,128)(2,1)S(1)}, bf16[128,512]{1,0:T(8,128)(2,1)}, u32[]{:S(2)}) %copy-start) | copy-done | bytes 131096
  1.6 28.6 %shard_map.37 = bf16[128,1792]{1,0:T(8,128)(2,1)S(1)} custom-call(bf16[128,1792]{1,0:T(8,128)(2,1)} %q_hbm.1, bf16[128,512]{1,0:T(8,128)(2,1)S(1)} %copy-done, s32[1,128]{1,0:T(1,128)S(1)} %bitcast.1), custom_call_target="tpu_custom_call" | custom-call | tf_op jit(solution)/shard_map/pallas_call | solution.py:377
  30.2 0.8 %copy.5 = bf16[128,1792]{1,0:T(8,128)(2,1)} copy(bf16[128,1792]{1,0:T(8,128)(2,1)S(1)} %shard_map.37) | data formatting | bytes 917504
Async XLA Ops:
  0.0 0.7 %copy-start.1 = (s32[128]{0:T(128)S(1)}, s32[128]{0:T(128)}, u32[]{:S(2)}) copy-start(s32[128]{0:T(128)} %param.5) | copy-start | bytes 1540
  0.7 0.9 %copy-start = (bf16[128,512]{1,0:T(8,128)(2,1)S(1)}, bf16[128,512]{1,0:T(8,128)(2,1)}, u32[]{:S(2)}) copy-start(bf16[128,512]{1,0:T(8,128)(2,1)} %kv_ref.1) | copy-start | bytes 393220

commit v7 on v6

--- a/solution.py
+++ b/solution.py
@@ -14,7 +14,7 @@
 MESH = pl.DeviceIdType.MESH
 
 
-def kernel(Z, Y, X, T, G, q_hbm, kv_ref, seg_ref, out_ref, q_ref, load, buf, stage, qrecv, qt, bias, mx, acc, ostage,
+def kernel(Z, Y, X, T, G, q_hbm, kv_hbm, seg_hbm, out_ref, q_ref, kv_ref, seg_ref, load, buf, stage, qrecv, qt, bias, mx, acc, ostage,
            pre_send, pre_recv, send, recv, out_send, out_recv):
     KR = T
     SR = T + 16
@@ -43,7 +43,11 @@
     def xprev(dx):
         return lax.rem(x - dx + X, X)
 
-    q_load = pltpu.make_async_copy(q_hbm.at[:, pl.ds(pl.multiple_of(c * W, HD), W)], q_ref, load)
+    q_load = pltpu.make_async_copy(q_hbm.at[:, pl.ds(pl.multiple_of(c * W, HD), W)], q_ref, load.at[0])
+    kv_load = pltpu.make_async_copy(kv_hbm, kv_ref, load.at[1])
+    seg_load = pltpu.make_async_copy(seg_hbm, seg_ref, load.at[2])
+    kv_load.start()
+    seg_load.start()
     q_load.start()
 
     barrier = pltpu.get_barrier_semaphore()
@@ -59,6 +63,9 @@
     @pl.when(z > 0)
     def _():
         pl.semaphore_signal(barrier, inc=1, device_id=at(z - 1, y, x), device_id_type=MESH)
+
+    kv_load.wait()
+    seg_load.wait()
 
     seg16 = jnp.broadcast_to(seg_ref[...].astype(jnp.float32), (16, T)).astype(jnp.bfloat16)
 
@@ -288,7 +295,7 @@
             return b, here
 
         def blocks(j, unused):
-            @pl.when(j == X // 2)
+            @pl.when((j == X // 2) & (s < z))
             def _():
                 pass_on(s)
 
@@ -306,6 +313,11 @@
             return unused
 
         lax.fori_loop(0, X, blocks, 0)
+
+        @pl.when(s == z)
+        def _():
+            pass_on(s)
+
         return unused
 
     lax.fori_loop(1, Z + 1, step, 0)
@@ -376,12 +388,14 @@
     dma = pltpu.SemaphoreType.DMA
     return pl.pallas_call(
         functools.partial(kernel, Z, Y, X, T, G),
-        out_shape=jax.ShapeDtypeStruct(queries.shape, jnp.bfloat16),
-        in_specs=[pl.BlockSpec(memory_space=pl.ANY), vmem, vmem],
+        out_shape=pltpu.VMEM(queries.shape, jnp.bfloat16),
+        in_specs=[pl.BlockSpec(memory_space=pl.ANY)] * 3,
         out_specs=vmem,
         scratch_shapes=[
             pltpu.VMEM((T, G * HD), jnp.bfloat16),
-            dma,
+            pltpu.VMEM(keys_values.shape, jnp.bfloat16),
+            pltpu.VMEM((1, T), jnp.int32),
+            dma((3,)),
             pltpu.VMEM((chips, 2, 2 * T + 16, HD), jnp.bfloat16),
             pltpu.VMEM((2 * T + 16, HD), jnp.bfloat16),
             pltpu.VMEM((T, G * HD), jnp.bfloat16),
@@ -398,7 +412,7 @@
             dma((G,)),
         ],
         compiler_params=pltpu.CompilerParams(
-            collective_id=0, has_side_effects=True, vmem_limit_bytes=53 * 1024 * 1024
+            collective_id=0, has_side_effects=True, vmem_limit_bytes=60 * 1024 * 1024
         ),
     )(queries, keys_values, segment_ids.reshape(1, T))
 

time: 31.1 us -> 31.4 us (level)
  Pallas kernels: 28.6 us -> 30.5 us
  local copies, waits for them, and re-layouts: 2.33 us -> 0.77 us
    pallas_call x1, Pallas kernels: 28.6 us -> 30.5 us  [shards(): pl.pallas_call(functools.partial(kernel, Z, Y, X, T, G), out_shape=pltpu....]
    unnamed x5 -> x1, local copies, waits for them, and re-layouts: 2.33 us -> 0.77 us
where the time goes in v7:
time: 31.4 us; the launch traced here: 31.2 us
  Pallas kernels  30.5 us (97%)
  local copies, waits for them, and re-layouts  0.77 us (2%)
    pallas_call x1, Pallas kernels, shards(): pl.pallas_call(functools.partial(kernel, Z, Y, X, T, G), out_shape=pltpu....  30.5 us
    unnamed x1, local copies, waits for them, and re-layouts  0.77 us

profile of v7, /device:TPU:25, one launch (start us, length us, event | category | flops | bytes accessed | tf_op | source)
XLA Modules:
  0.0 31.2 jit_solution(4994194651289399984)
XLA Ops:
  0.0 30.5 %shard_map.37 = bf16[128,1792]{1,0:T(8,128)(2,1)S(1)} custom-call(bf16[128,1792]{1,0:T(8,128)(2,1)} %q_hbm.1, bf16[128,512]{1,0:T(8,128)(2,1)} %kv_hbm.1, s32[1,128]{1,0:T(1,128)} %bitcast.1), custom_call_target="tpu_custom_call" | custom-call | tf_op jit(solution)/shard_map/pallas_call | solution.py:389
  30.5 0.8 %copy.5 = bf16[128,1792]{1,0:T(8,128)(2,1)} copy(bf16[128,1792]{1,0:T(8,128)(2,1)S(1)} %shard_map.37) | data formatting | bytes 917504

commit v8 on v6

--- a/solution.py
+++ b/solution.py
@@ -115,7 +115,7 @@
     def for_plane(b, zz):
         return b >= zz * Y * X - reach
 
-    def send_half(s, half):
+    def lift(s, half):
         b = number(z - s, y, x)
 
         @pl.when((s > 0) & for_plane(b, z))
@@ -126,9 +126,15 @@
         def _():
             copy(half, s, b, half, up, s + 1).start()
 
+    def send_y(s, half):
+        b = number(z - s, y, x)
+
         @pl.when(for_row(b, 1 - y, half))
         def _():
             copy(2 + half, s, b, half, side).start()
+
+    def send_x(s, half):
+        b = number(z - s, y, x)
 
         for dx in range(1, X):
             @pl.when(for_column(b, xnext(dx), half))
@@ -158,11 +164,20 @@
             def _():
                 copy(onward_y(dx), s, e, 1, side).start()
 
+    def send_half(s, half):
+        lift(s, half)
+        send_y(s, half)
+        send_x(s, half)
+
     def pass_up(s):
         @pl.when(s <= z)
         def _():
-            send_half(s, 0)
-            send_half(s, 1)
+            lift(s, 0)
+            send_y(s, 0)
+            lift(s, 1)
+            send_x(s, 1)
+            send_y(s, 1)
+            send_x(s, 0)
 
     def pass_on(s):
         @pl.when(s <= z)

time: 31.1 us -> 31.3 us (level)
  no operation moved by 1% of the time
where the time goes in v8:
time: 31.3 us; the launch traced here: 31.2 us
  Pallas kernels  28.8 us (92%)
  local copies, waits for them, and re-layouts  2.33 us (7%)
    pallas_call x1, Pallas kernels, shards(): pl.pallas_call(functools.partial(kernel, Z, Y, X, T, G), out_shape=jax.Sh...  28.8 us
    unnamed x5, local copies, waits for them, and re-layouts  2.33 us

profile of v8, /device:TPU:25, one launch (start us, length us, event | category | flops | bytes accessed | tf_op | source)
XLA Modules:
  0.0 31.2 jit_solution(3562955929094498235)
XLA Ops:
  0.0 0.0 copy-start.1
  0.0 0.7 %copy-done.1 = s32[128]{0:T(128)S(1)} copy-done((s32[128]{0:T(128)S(1)}, s32[128]{0:T(128)}, u32[]{:S(2)}) %copy-start.1) | copy-done | bytes 536
  0.7 0.0 copy-start
  0.7 0.9 %copy-done = bf16[128,512]{1,0:T(8,128)(2,1)S(1)} copy-done((bf16[128,512]{1,0:T(8,128)(2,1)S(1)}, bf16[128,512]{1,0:T(8,128)(2,1)}, u32[]{:S(2)}) %copy-start) | copy-done | bytes 131096
  1.6 28.8 %shard_map.37 = bf16[128,1792]{1,0:T(8,128)(2,1)S(1)} custom-call(bf16[128,1792]{1,0:T(8,128)(2,1)} %q_hbm.1, bf16[128,512]{1,0:T(8,128)(2,1)S(1)} %copy-done, s32[1,128]{1,0:T(1,128)S(1)} %bitcast.1), custom_call_target="tpu_custom_call" | custom-call | tf_op jit(solution)/shard_map/pallas_call | solution.py:392
  30.4 0.8 %copy.5 = bf16[128,1792]{1,0:T(8,128)(2,1)} copy(bf16[128,1792]{1,0:T(8,128)(2,1)S(1)} %shard_map.37) | data formatting | bytes 917504
Async XLA Ops:
  0.0 0.7 %copy-start.1 = (s32[128]{0:T(128)S(1)}, s32[128]{0:T(128)}, u32[]{:S(2)}) copy-start(s32[128]{0:T(128)} %param.5) | copy-start | bytes 1540
  0.7 0.9 %copy-start = (bf16[128,512]{1,0:T(8,128)(2,1)S(1)}, bf16[128,512]{1,0:T(8,128)(2,1)}, u32[]{:S(2)}) copy-start(bf16[128,512]{1,0:T(8,128)(2,1)} %kv_ref.1) | copy-start | bytes 393220

commit v9 on v6

--- a/solution.py
+++ b/solution.py
@@ -68,6 +68,9 @@
         ref[SR:, :] = kv_ref[:, pl.ds(pl.multiple_of((KVH + h) * HD, HD), HD)].T
 
     piece(stage, o)
+    piece(buf.at[me, c], c)
+    for g in range(G):
+        qt[HD + 16:, g * C:(g + 1) * C] = jnp.zeros((HD - 16, C), jnp.bfloat16)
     pl.semaphore_wait(
         barrier, 2 + NX + jnp.where(z < Z - 1, 1, 0) + jnp.where(z > 0, 1, 0)
     )
@@ -83,7 +86,6 @@
         q_hbm.at[:, pl.ds(pl.multiple_of(o * W, HD), W)], qrecv, pre_send.at[1], pre_recv.at[1], sibling
     )
     q_swap.start()
-    piece(buf.at[me, c], c)
 
     def number(zz, yy, xx):
         return (zz * Y + yy) * X + xx
@@ -189,7 +191,6 @@
     top16 = jnp.where(rows == 0, -BIG, jnp.where(rows == 1, hidden, 0.0)).astype(jnp.bfloat16)
     for g in range(G):
         qt[HD:HD + 16, g * C:(g + 1) * C] = top16
-        qt[HD + 16:, g * C:(g + 1) * C] = jnp.zeros((HD - 16, C), jnp.bfloat16)
     turned = [jnp.broadcast_to(s[0:1, :], (T, T)).T for s in (seg0, seg1)]
     seg_k = jnp.concatenate(turned, axis=0)
     seg_k = jnp.concatenate([seg_k, seg_k], axis=1)
@@ -315,11 +316,13 @@
     swaps = []
     for g in range(G):
         place = out_ref.at[:, pl.ds(pl.multiple_of(c * W + g * HD, HD), HD)]
-        ostage[g] = (acc[g, 0:HD, theirs] / acc[g, HD:HD + 1, theirs]).astype(jnp.bfloat16).T
+        ostage[g] = (acc[g, 0:HD, theirs] * (1.0 / acc[g, HD:HD + 1, theirs])).astype(jnp.bfloat16).T
         swap = remote(ostage.at[g], place, out_send.at[g], out_recv.at[g], sibling)
         swap.start()
         swaps.append(swap)
-        place[...] = (acc[g, 0:HD, mine] / acc[g, HD:HD + 1, mine]).astype(jnp.bfloat16).T
+    for g in range(G):
+        place = out_ref.at[:, pl.ds(pl.multiple_of(c * W + g * HD, HD), HD)]
+        place[...] = (acc[g, 0:HD, mine] * (1.0 / acc[g, HD:HD + 1, mine])).astype(jnp.bfloat16).T
 
     def drain(s, unused):
         @pl.when(s <= z)

time: 31.1 us -> 30.8 us (level)
  no operation moved by 1% of the time
where the time goes in v9:
time: 30.8 us; the launch traced here: 30.7 us
  Pallas kernels  28.4 us (92%)
  local copies, waits for them, and re-layouts  2.33 us (8%)
    pallas_call x1, Pallas kernels, shards(): pl.pallas_call(functools.partial(kernel, Z, Y, X, T, G), out_shape=jax.Sh...  28.4 us
    unnamed x5, local copies, waits for them, and re-layouts  2.33 us

profile of v9, /device:TPU:25, one launch (start us, length us, event | category | flops | bytes accessed | tf_op | source)
XLA Modules:
  0.0 30.7 jit_solution(13431787602887877887)
XLA Ops:
  0.0 0.0 copy-start.1
  0.0 0.7 %copy-done.1 = s32[128]{0:T(128)S(1)} copy-done((s32[128]{0:T(128)S(1)}, s32[128]{0:T(128)}, u32[]{:S(2)}) %copy-start.1) | copy-done | bytes 536
  0.7 0.0 copy-start
  0.7 0.9 %copy-done = bf16[128,512]{1,0:T(8,128)(2,1)S(1)} copy-done((bf16[128,512]{1,0:T(8,128)(2,1)S(1)}, bf16[128,512]{1,0:T(8,128)(2,1)}, u32[]{:S(2)}) %copy-start) | copy-done | bytes 131096
  1.6 28.4 %shard_map.37 = bf16[128,1792]{1,0:T(8,128)(2,1)S(1)} custom-call(bf16[128,1792]{1,0:T(8,128)(2,1)} %q_hbm.1, bf16[128,512]{1,0:T(8,128)(2,1)S(1)} %copy-done, s32[1,128]{1,0:T(1,128)S(1)} %bitcast.1), custom_call_target="tpu_custom_call" | custom-call | tf_op jit(solution)/shard_map/pallas_call | solution.py:380
  29.9 0.8 %copy.5 = bf16[128,1792]{1,0:T(8,128)(2,1)} copy(bf16[128,1792]{1,0:T(8,128)(2,1)S(1)} %shard_map.37) | data formatting | bytes 917504
Async XLA Ops:
  0.0 0.7 %copy-start.1 = (s32[128]{0:T(128)S(1)}, s32[128]{0:T(128)}, u32[]{:S(2)}) copy-start(s32[128]{0:T(128)} %param.5) | copy-start | bytes 1540
  0.7 0.9 %copy-start = (bf16[128,512]{1,0:T(8,128)(2,1)S(1)}, bf16[128,512]{1,0:T(8,128)(2,1)}, u32[]{:S(2)}) copy-start(bf16[128,512]{1,0:T(8,128)(2,1)} %kv_ref.1) | copy-start | bytes 393220
